TPU v7x, 512 devices: a whole 4x4x16 slice. The times are simulated.
512 devices in a mesh: rows: 128 (over x, y_hi, z), snap: 4 (over y_lo, core).
Axes of the slice: x: 4, y: 4 (y_hi: 2, y_lo: 2; y = y_hi * 2 + y_lo), z: 16, core: 2. Of those that a mesh axis runs over, the one named last changes fastest.
Arguments:
- snapshots: float32 [98304, 2048], P('rows', 'snap'), may hold values from -5000 to 5000
Outputs:
- correlation: float32 [2048, 2048], P('snap', 'rows')
All inputs are finite; a program needn't handle non-finite values.
Results may differ from a plain program's by a relative error of at most 0.00026.
Values sent between devices are 32-bit elements; how exact they have to be, the bound alone decides.
A program may use at most 64 MiB of HBM per device.

v0:
```python
import jax
import jax.numpy as jnp
from jax import lax
from jax.sharding import PartitionSpec as P

eps = 1e-06


def passed_along(block, axis, distance):
    devices = range(lax.axis_size(axis))
    route = [((i - distance) % len(devices), i) for i in devices]
    return lax.ppermute(block, axis, route)


def per_device(snapshots):
    block_width = snapshots.shape[1]
    cycle_size = lax.axis_size("snap")
    snap_total = block_width * cycle_size
    position = lax.axis_index("snap")
    row_total = lax.psum(jnp.sum(snapshots, axis=1), "snap")
    fluctuation = snapshots - (row_total / snap_total)[:, None]
    gram_slots = [None] * cycle_size

    def record(slot, visiting):
        gram_slots[slot] = lax.dot_general(
            fluctuation,
            visiting,
            (((0,), (0,)), ((), ())),
            precision=lax.Precision.HIGHEST,
            preferred_element_type=jnp.float32,
        )

    record(0, fluctuation)
    visiting = fluctuation
    for step in range(1, cycle_size):
        visiting = passed_along(visiting, "snap", 1)
        record(-step % cycle_size, visiting)
    gram_part = jnp.roll(jnp.stack(gram_slots, axis=1), position, axis=1).reshape(
        block_width, snap_total
    )
    gram_owned = lax.psum_scatter(gram_part, "rows", scatter_dimension=1, tiled=True)
    owned_cols = gram_owned.shape[1]
    energy_own = lax.psum(jnp.sum(fluctuation * fluctuation, axis=0), "rows")
    energy_all = lax.all_gather(energy_own, "snap", axis=0, tiled=True)
    energy_cols = lax.dynamic_slice_in_dim(
        energy_all, lax.axis_index("rows") * owned_cols, owned_cols
    )
    return gram_owned * lax.rsqrt(energy_own + eps)[:, None] * lax.rsqrt(energy_cols + eps)[None, :]


def solution(mesh):
    in_specs = (P("rows", "snap"),)
    out_specs = P("snap", "rows")
    return jax.shard_map(
        per_device, mesh=mesh, in_specs=in_specs, out_specs=out_specs, check_vma=False
    )
```

profile of v0, /device:TPU:8, one launch (start us, length us, event | category | flops | bytes accessed | tf_op | source)
XLA Modules:
  0.0 833.3 jit_solution(3739338906207116380)
XLA Ops:
  6.5 0.0 copy-start
  6.5 0.0 reduce-scatter.2.cloned.1.call-start
  6.5 1.7 reduce_sum.18
  8.2 9.4 %psum.14 = f32[768]{0:T(1024)S(1)} all-reduce(f32[768]{0:T(1024)S(1)} %reduce_sum.18), channel_id=1, replica_groups=mesh['rows'=128,'snap'=4] {'snap'}, use_global_device_ids=true, to_apply=%region_1.0 | all-reduce | flops 768 | bytes 6144 | tf_op jit(solution)/shard_map/psum | solution.py:20
  17.6 0.0 copy-done
  17.6 0.3 multiply_reduce_fusion
  17.9 2.3 collective-permute-start
  20.2 19.5 %collective-permute-done = f32[768,512]{1,0:T(8,128)S(1)} collective-permute-done((f32[768,512]{1,0:T(8,128)S(1)}, f32[768,512]{1,0:T(8,128)S(1)}, u32[]{:S(2)}, u32[]{:S(2)}) %collective-permute-start) | collective-permute-done | bytes 1572896 | tf_op jit(solution)/shard_map/ppermute | solution.py:12
  39.6 1.9 collective-permute-start.1
  41.5 19.9 %collective-permute-done.1 = f32[768,512]{1,0:T(8,128)} collective-permute-done((f32[768,512]{1,0:T(8,128)S(1)}, f32[768,512]{1,0:T(8,128)}, u32[]{:S(2)}, u32[]{:S(2)}) %collective-permute-start.1) | collective-permute-done | bytes 1572896 | tf_op jit(solution)/shard_map/ppermute | solution.py:12
  61.5 1.9 collective-permute-start.2
  63.4 2.7 constant_dynamic-update-slice_fusion.7
  66.1 17.4 %collective-permute-done.2 = f32[768,512]{1,0:T(8,128)} collective-permute-done((f32[768,512]{1,0:T(8,128)}, f32[768,512]{1,0:T(8,128)}, u32[]{:S(2)}, u32[]{:S(2)}) %collective-permute-start.2) | collective-permute-done | bytes 1572896 | tf_op jit(solution)/shard_map/ppermute | solution.py:12
  83.5 4.1 constant_dynamic-update-slice_fusion.6
  87.6 4.1 constant_dynamic-update-slice_fusion.5
  91.7 2.7 constant_dynamic-update-slice_fusion.4
  94.5 0.1 constant_dynamic-update-slice_fusion.3
  94.5 0.1 constant_dynamic-update-slice_fusion.2
  94.6 0.1 constant_dynamic-update-slice_fusion.1
  94.7 0.1 constant_dynamic-update-slice_fusion
  94.8 2.4 constant_dynamic-slice_fusion
  97.1 0.0 reduce-scatter.2.cloned.1.call-update
  97.2 361.9 %psum.15 = f32[512]{0:T(512)S(1)} all-reduce(f32[512]{0:T(512)S(1)} %get-tuple-element.5), channel_id=1, replica_groups=mesh['rows'=128,'snap'=4] {'rows'}, use_global_device_ids=true, to_apply=%region_4.5 | all-reduce | flops 512 | bytes 4096 | tf_op jit(solution)/shard_map/psum | solution.py:43
  459.1 5.1 all-gather
  464.3 0.1 add_rsqrt_fusion.1
  464.3 360.7 %reduce-scatter.2.cloned.1.call-done = f32[512,16]{0,1:T(8,128)} async-done(((f32[512,2048]{0,1:T(8,128)}), f32[512,16]{0,1:T(8,128)}) %reduce-scatter.2.cloned.1.call-update) | async-done | bytes 32784 | tf_op jit(solution)/shard_map/reduce_scatter | solution.py:41
  825.0 1.4 multiply_multiply_fusion
  (2 shorter events, 0.0 us)
Async XLA Ops:
  6.5 11.1 %copy-start = (f32[768,512]{1,0:T(8,128)S(1)}, f32[768,512]{1,0:T(8,128)}, u32[]{:S(2)}) copy-start(f32[768,512]{1,0:T(8,128)} %param.1) | copy-start | bytes 4718596
  6.5 818.5 %reduce-scatter.2.cloned.1.call-start = ((), (), s32[]{:S(2)}) async-start(), calls=%async_computation.1 | async-start | bytes 4227072 | tf_op jit(solution)/shard_map/reduce_scatter | solution.py:41
  17.9 21.7 %collective-permute-start = (f32[768,512]{1,0:T(8,128)S(1)}, f32[768,512]{1,0:T(8,128)S(1)}, u32[]{:S(2)}, u32[]{:S(2)}) collective-permute-start(f32[768,512]{1,0:T(8,128)S(1)} %get-tuple-element.6), channel_id=1, source_target_pairs={{3,0},{0,1},{1,2},{2,3},{7,4},{4,5},{5,6},{6,7},{11,8},{8,9},{9,10... | collective-permute-start | bytes 4718600 | tf_op jit(solution)/shard_map/ppermute | solution.py:12
  39.6 21.8 %collective-permute-start.1 = (f32[768,512]{1,0:T(8,128)S(1)}, f32[768,512]{1,0:T(8,128)}, u32[]{:S(2)}, u32[]{:S(2)}) collective-permute-start(f32[768,512]{1,0:T(8,128)S(1)} %collective-permute-done), channel_id=1, source_target_pairs={{3,0},{0,1},{1,2},{2,3},{7,4},{4,5},{5,6},{6,7},{11,8},{8,9},{9,10... | collective-permute-start | bytes 4718600 | tf_op jit(solution)/shard_map/ppermute | solution.py:12
  61.5 22.0 %collective-permute-start.2 = (f32[768,512]{1,0:T(8,128)}, f32[768,512]{1,0:T(8,128)}, u32[]{:S(2)}, u32[]{:S(2)}) collective-permute-start(f32[768,512]{1,0:T(8,128)} %collective-permute-done.1), channel_id=1, source_target_pairs={{3,0},{0,1},{1,2},{2,3},{7,4},{4,5},{5,6},{6,7},{11,8},{8,9},{9,10... | collective-permute-start | bytes 4718600 | tf_op jit(solution)/shard_map/ppermute | solution.py:12
Sparse Core Ops, SparseCore 0:
  97.3 727.7 reduce-scatter.1
where the time goes:
time: 834 us; the launch traced here: 833 us
  waiting for transfers between devices  417 us (50%)
  blocking collectives  376 us (45%)
  matrix products  13.6 us (2%)
  between operations  13.5 us (2%)
    psum x1, blocking collectives, per_device(): energy_own = lax.psum(jnp.sum(fluctuation * fluctuation, axis=0), 'rows')  362 us
    reduce_scatter x1, waiting for transfers between devices, per_device(): lax.psum_scatter(gram_part, 'rows', scatter_dimension=1, tiled=True)  361 us
    ppermute x3, waiting for transfers between devices, passed_along(): return lax.ppermute(block, axis, route)  56.8 us
  transfers between devices with their start and end apart: 4, of which 4 were waited for; matrix products, arithmetic and copies ran while one was open for 0% of the time, Pallas kernels for 0%

commit v1 on v0

v1 whole, which is shorter than its diff:
```python
import jax
import jax.numpy as jnp
from jax import lax
from jax.experimental import pallas as pl
from jax.experimental.pallas import tpu as pltpu
from jax.sharding import PartitionSpec as P

eps = 1e-06
MESH = pl.DeviceIdType.MESH
f32, bf16 = jnp.float32, jnp.bfloat16

NX, NH, NZ = 4, 2, 16
ROWS, COLS = 768, 512
HALF = ROWS // 2
TILE = 128
SNAPS = 2048
ZR, ZL = NZ // 2, NZ // 2 - 1


def device(x, h, z, low, core):
    return ((x * NH + h) * NZ + z, low * 2 + core)


def kernel(
    x_ref, out_ref,
    other, cross, sums, mean, hi, lo, t_hi, t_lo, c_hi, c_lo,
    aa, ab, unit, from_left, from_right,
    unit_r, unit_l, ab_r, ab_l,
    e_own, e_r, e_l, e_x, e_sum, e_h, e_all, e_col,
    held, flip, direct, turned,
    core_ss, core_rs, y_ss, y_rs, relay_ss, relay_rs, sum_ss, sum_rs,
    xr_ss, xr_rs, xl_ss, xl_rs,
    ur_ss, ur_rs, ul_ss, ul_rs, abr_ss, abr_rs, abl_ss, abl_rs,
    er_ss, er_rs, el_ss, el_rs, ex_ss, ex_rs, eh_ss, eh_rs, eg_ss, eg_rs,
    fin_ss, fin_rs,
):
    r, s = lax.axis_index("rows"), lax.axis_index("snap")
    x, h, z = r // (NH * NZ), (r // NZ) % NH, r % NZ
    low, core = s // 2, s % 2
    zr, zl = device(x, h, (z + 1) % NZ, low, core), device(x, h, (z + NZ - 1) % NZ, low, core)
    xr, xl = device((x + 1) % NX, h, z, low, core), device((x + NX - 1) % NX, h, z, low, core)
    xx = device((x + 2) % NX, h, z, low, core)
    hh = device(x, 1 - h, z, low, core)
    twin = device(x, h, z, low, 1 - core)
    pair = device(x, h, z, 1 - low, core)
    diagonal = device(x, h, z, 1 - low, 1 - core)
    group = (twin, pair, diagonal)
    pending = []

    def send(src, dst, send_sem, recv_sem, target):
        copy = pltpu.make_async_remote_copy(
            src_ref=src, dst_ref=dst, send_sem=send_sem, recv_sem=recv_sem,
            device_id=target, device_id_type=MESH,
        )
        copy.start()
        pending.append((src, send_sem))
        return copy

    def arrived(dst, sem):
        pltpu.make_async_copy(dst, dst, sem).wait()

    barrier = pltpu.get_barrier_semaphore()
    near = (twin, pair, diagonal, zr, zl, xr, xl, xx, hh)
    for target in near:
        pl.semaphore_signal(barrier, inc=1, device_id=target, device_id_type=MESH)

    for q in range(ROWS // TILE):
        block = x_ref[q * TILE:(q + 1) * TILE, :]
        part = block[:, 0:128] + block[:, 128:256] + block[:, 256:384] + block[:, 384:512]
        sums[s, q:q + 1, :] = jnp.sum(part.T, axis=0, keepdims=True)
    sums[s, 6:8, :] = jnp.zeros((2, TILE), f32)
    pl.semaphore_wait(barrier, len(near))

    for i, target in enumerate(group):
        send(sums.at[s], sums.at[s], sum_ss.at[i], sum_rs.at[i], target)
    send(x_ref, other, core_ss, core_rs, twin)
    give = pl.multiple_of((1 - low) * HALF, HALF)
    send(x_ref.at[pl.ds(give, HALF)], cross.at[0], y_ss, y_rs, pair)

    for i, d in enumerate((s ^ 1, s ^ 2, s ^ 3)):
        arrived(sums.at[d], sum_rs.at[i])
    mean_rows = (sums[0] + sums[1] + sums[2] + sums[3]) / SNAPS
    for q in range(ROWS // TILE):
        wide = jnp.broadcast_to(mean_rows[q:q + 1, :], (TILE, TILE))
        mean[q * TILE:(q + 1) * TILE, :] = wide.T

    def split(value):
        high = value.astype(bf16)
        return high, (value - high.astype(f32)).astype(bf16)

    def turn(block, q, to_hi, to_lo, j):
        high, rest = split(block.T)
        to_hi[j * TILE:(j + 1) * TILE, pl.ds(q * TILE, TILE)] = high
        to_lo[j * TILE:(j + 1) * TILE, pl.ds(q * TILE, TILE)] = rest

    energy = [jnp.zeros((8, TILE), f32) for _ in range(4)]
    for q in range(ROWS // TILE):
        rows = slice(q * TILE, (q + 1) * TILE)
        for j in range(4):
            block = x_ref[rows, j * TILE:(j + 1) * TILE] - mean[rows, :]
            energy[j] += jnp.sum((block * block).reshape(TILE // 8, 8, TILE), axis=0)
            high, rest = split(block)
            hi[rows, j * TILE:(j + 1) * TILE] = high
            lo[rows, j * TILE:(j + 1) * TILE] = rest
            turn(block, q, t_hi.at[0], t_lo.at[0], j)
    for j in range(4):
        e_own[j:j + 1, :] = jnp.sum(energy[j], axis=0, keepdims=True)
    e_own[4:8, :] = jnp.zeros((4, TILE), f32)

    def e_step(t):
        if t > 0:
            arrived(e_r.at[t - 1], er_rs.at[t - 1])
        if t < ZR:
            send(e_own if t == 0 else e_r.at[t - 1], e_r.at[t], er_ss.at[t], er_rs.at[t], zr)
        if 0 < t <= ZL:
            arrived(e_l.at[t - 1], el_rs.at[t - 1])
        if t < ZL:
            send(e_own if t == 0 else e_l.at[t - 1], e_l.at[t], el_ss.at[t], el_rs.at[t], zl)

    e_step(0)

    def product(a_hi, a_lo, b_hi, b_lo):
        total = jnp.dot(a_hi, b_hi, preferred_element_type=f32)
        total += jnp.dot(a_hi, b_lo, preferred_element_type=f32)
        return total + jnp.dot(a_lo, b_hi, preferred_element_type=f32)

    def own_chip(side, owner):
        @pl.loop(0, 2)
        def _(half):
            at = pl.ds(pl.multiple_of(half * 256, 256), 256)
            got = product(t_hi[side, at, :], t_lo[side, at, :], hi[...], lo[...])
            aa[owner * 2 + half] = got.reshape(NZ, 16, COLS)

    own_chip(0, core)
    arrived(other, core_rs)
    for q in range(ROWS // TILE):
        rows = slice(q * TILE, (q + 1) * TILE)
        for j in range(4):
            turn(other[rows, j * TILE:(j + 1) * TILE] - mean[rows, :], q, t_hi.at[1], t_lo.at[1], j)
    own_chip(1, 1 - core)

    a_half, b_half = pl.ds(0, ZR), pl.ds(ZR, ZR)
    far, right, left = (x + 2) % NX, (x + 1) % NX, (x + NX - 1) % NX
    send(aa.at[far, a_half], from_left.at[0], xr_ss.at[0], xr_rs.at[0], xr)
    send(aa.at[far, b_half], from_right.at[0], xl_ss.at[0], xl_rs.at[0], xl)
    send(aa.at[right, b_half], from_left.at[1], xr_ss.at[1], xr_rs.at[1], xr)
    send(aa.at[left, a_half], from_right.at[1], xl_ss.at[1], xl_rs.at[1], xl)
    for t in range(1, 4):
        e_step(t)
    arrived(from_left.at[0], xr_rs.at[0])
    from_left[0] = from_left[0] + aa[right, a_half]
    send(from_left.at[0], from_left.at[2], xr_ss.at[2], xr_rs.at[2], xr)
    arrived(from_right.at[0], xl_rs.at[0])
    from_right[0] = from_right[0] + aa[left, b_half]
    send(from_right.at[0], from_right.at[2], xl_ss.at[2], xl_rs.at[2], xl)
    for t in range(4, ZR + 1):
        e_step(t)
    e_x[3] = e_own[...] + jnp.sum(e_r[...], axis=0) + jnp.sum(e_l[...], axis=0)
    for i, target in enumerate((xr, xl, xx)):
        send(e_x.at[3], e_x.at[i], ex_ss.at[i], ex_rs.at[i], target)

    keep = pl.multiple_of(low * HALF, HALF)

    def cross_chip(side):
        for q in range(HALF // TILE):
            rows = slice(q * TILE, (q + 1) * TILE)
            level = mean[pl.ds(keep + q * TILE, TILE), :]
            for j in range(4):
                turn(cross[side, rows, j * TILE:(j + 1) * TILE] - level, q, c_hi.at[side], c_lo.at[side], j)

        @pl.loop(0, 4)
        def _(tile):
            at = pl.ds(pl.multiple_of(tile * TILE, TILE), TILE)
            got = product(c_hi[side, at, :], c_lo[side, at, :],
                          hi[pl.ds(keep, HALF), :], lo[pl.ds(keep, HALF), :])
            for j in range(4):
                ab[side, tile * 4 + j] = got[:, j * TILE:(j + 1) * TILE]

    def z_step(t, part, slots_r, slots_l, ssr, rsr, ssl, rsl):
        to_r, to_l = (z + ZR - t + NZ) % NZ, (z + NZ - ZL + t) % NZ
        if 0 < t < ZR:
            arrived(slots_r.at[t - 1], rsr.at[t - 1])
            slots_r[t - 1] = slots_r[t - 1] + part[to_r]
        if t < ZR:
            src = part.at[to_r] if t == 0 else slots_r.at[t - 1]
            send(src, slots_r.at[t], ssr.at[t], rsr.at[t], zr)
        if 0 < t < ZL:
            arrived(slots_l.at[t - 1], rsl.at[t - 1])
            slots_l[t - 1] = slots_l[t - 1] + part[to_l]
        if t < ZL:
            src = part.at[to_l] if t == 0 else slots_l.at[t - 1]
            send(src, slots_l.at[t], ssl.at[t], rsl.at[t], zl)

    def z_last(part, slots_r, slots_l, rsr, rsl):
        arrived(slots_r.at[ZR - 1], rsr.at[ZR - 1])
        arrived(slots_l.at[ZL - 1], rsl.at[ZL - 1])
        return part[z] + slots_r[ZR - 1] + slots_l[ZL - 1]

    def unit_step(t):
        z_step(t, unit, unit_r, unit_l, ur_ss, ur_rs, ul_ss, ul_rs)

    def cross_step(t, side):
        z_step(t, ab.at[side], ab_r.at[side], ab_l.at[side],
               abr_ss.at[side], abr_rs.at[side], abl_ss.at[side], abl_rs.at[side])

    arrived(cross.at[0], y_rs)
    send(cross.at[0], cross.at[1], relay_ss, relay_rs, twin)
    cross_chip(0)
    cross_step(0, 0)

    arrived(from_left.at[1], xr_rs.at[1])
    arrived(from_right.at[1], xl_rs.at[1])
    arrived(from_left.at[2], xr_rs.at[2])
    arrived(from_right.at[2], xl_rs.at[2])
    unit[a_half] = aa[x, a_half] + from_left[2] + from_right[1]
    unit[b_half] = aa[x, b_half] + from_left[1] + from_right[2]
    unit_step(0)

    arrived(cross.at[1], relay_rs)
    cross_chip(1)
    cross_step(0, 1)

    for i in range(3):
        arrived(e_x.at[i], ex_rs.at[i])
    e_sum[...] = e_x[0] + e_x[1] + e_x[2] + e_x[3]
    send(e_sum, e_h, eh_ss, eh_rs, hh)
    for t in range(1, 3):
        cross_step(t, 0)
        unit_step(t)
        cross_step(t, 1)
    arrived(e_h, eh_rs)
    e_all[s] = e_sum[...] + e_h[...]
    for i, target in enumerate(group):
        send(e_all.at[s], e_all.at[s], eg_ss.at[i], eg_rs.at[i], target)
    for t in range(3, ZR):
        cross_step(t, 0)
        unit_step(t)
        cross_step(t, 1)
    for i, d in enumerate((s ^ 1, s ^ 2, s ^ 3)):
        arrived(e_all.at[d], eg_rs.at[i])

    held[...] = z_last(unit, unit_r, unit_l, ur_rs, ul_rs)
    to_x, to_h = 2 * low + x // 2, x % 2
    mine = jnp.logical_and(to_x == x, to_h == h)

    @pl.when(mine)
    def _():
        pltpu.make_async_copy(held, direct.at[h], fin_rs.at[0]).start()

    @pl.when(jnp.logical_not(mine))
    def _():
        pltpu.make_async_remote_copy(
            src_ref=held, dst_ref=direct.at[h], send_sem=fin_ss.at[0], recv_sem=fin_rs.at[0],
            device_id=device(to_x, to_h, z, low, core), device_id_type=MESH,
        ).start()

    row_tile, lane_tile = z // 4, z % 4
    me = x * NH + h
    for side in range(2):
        block = z_last(ab.at[side], ab_r.at[side], ab_l.at[side], abr_rs.at[side], abl_rs.at[side])
        flip[side, 0] = block
        flip[side, 1] = block.T
        their = core if side == 0 else 1 - core

        @pl.loop(0, 8)
        def _(k):
            src = pl.ds(pl.multiple_of(k * 16, 16), 16)
            lanes = pl.ds(pl.multiple_of(lane_tile * TILE, TILE), TILE)
            ox, oh, oz = 2 * (1 - low) + their, row_tile // 2, (row_tile % 2) * 8 + k
            own = jnp.logical_and(ox == x, jnp.logical_and(oh == h, oz == z))

            @pl.when(own)
            def _():
                pltpu.make_async_copy(flip.at[side, 0, src], direct.at[me, :, lanes], fin_rs.at[0]).start()

            @pl.when(jnp.logical_not(own))
            def _():
                pltpu.make_async_remote_copy(
                    src_ref=flip.at[side, 0, src], dst_ref=direct.at[me, :, lanes],
                    send_sem=fin_ss.at[1 + side * 16 + k], recv_sem=fin_rs.at[0],
                    device_id=device(ox, oh, oz, low, core), device_id_type=MESH,
                ).start()

            wide = pl.ds(pl.multiple_of(row_tile * TILE, TILE), TILE)
            pltpu.make_async_remote_copy(
                src_ref=flip.at[side, 1, src], dst_ref=turned.at[me, :, wide],
                send_sem=fin_ss.at[9 + side * 16 + k], recv_sem=fin_rs.at[1],
                device_id=device(2 * low + core, lane_tile // 2, (lane_tile % 2) * 8 + k, 1 - low, their),
                device_id_type=MESH,
            ).start()

    line = h * 2 + z // 8
    e_col[...] = jnp.broadcast_to(e_all[x, pl.ds(line, 1), :], (TILE, TILE)).T
    scale_j = lax.rsqrt(e_col[pl.ds(pl.multiple_of((z % 8) * 16, 16), 16), :] + eps)
    scale_i = lax.rsqrt(e_all[s] + eps)

    def finish(total):
        for j in range(4):
            lanes = slice(j * TILE, (j + 1) * TILE)
            out_ref[:, lanes] = total[:, lanes] * scale_i[j:j + 1, :] * scale_j

    @pl.when(x // 2 == low)
    def _():
        arrived(direct.at[pl.ds(0, 2)], fin_rs.at[0])
        finish(direct[0] + direct[1])

    @pl.when(x // 2 != low)
    def _():
        arrived(direct, fin_rs.at[0])
        arrived(turned, fin_rs.at[1])
        finish(jnp.sum(direct[...], axis=0) + jnp.sum(turned[...], axis=0))

    for src, sem in pending:
        arrived(src, sem)

    @pl.when(jnp.logical_not(mine))
    def _():
        arrived(held, fin_ss.at[0])

    for side in range(2):
        their = core if side == 0 else 1 - core

        @pl.loop(0, 8)
        def _(k):
            src = flip.at[side, 0, pl.ds(0, 16)]
            ox, oh, oz = 2 * (1 - low) + their, row_tile // 2, (row_tile % 2) * 8 + k
            own = jnp.logical_and(ox == x, jnp.logical_and(oh == h, oz == z))

            @pl.when(jnp.logical_not(own))
            def _():
                arrived(src, fin_ss.at[1 + side * 16 + k])

            arrived(src, fin_ss.at[9 + side * 16 + k])


def per_device(snapshots):
    dma = pltpu.SemaphoreType.DMA
    vmem = pltpu.VMEM
    strip = pl.pallas_call(
        kernel,
        out_shape=jax.ShapeDtypeStruct((16, COLS), f32),
        in_specs=[pl.BlockSpec(memory_space=pltpu.VMEM)],
        out_specs=pl.BlockSpec(memory_space=pltpu.VMEM),
        scratch_shapes=[
            vmem((ROWS, COLS), f32),
            vmem((2, HALF, COLS), f32),
            vmem((4, 8, TILE), f32),
            vmem((ROWS, TILE), f32),
            vmem((ROWS, COLS), bf16), vmem((ROWS, COLS), bf16),
            vmem((2, COLS, ROWS), bf16), vmem((2, COLS, ROWS), bf16),
            vmem((2, COLS, HALF), bf16), vmem((2, COLS, HALF), bf16),
            vmem((4, NZ, 16, COLS), f32),
            vmem((2, NZ, TILE, TILE), f32),
            vmem((NZ, 16, COLS), f32),
            vmem((3, ZR, 16, COLS), f32), vmem((3, ZR, 16, COLS), f32),
            vmem((ZR, 16, COLS), f32), vmem((ZL, 16, COLS), f32),
            vmem((2, ZR, TILE, TILE), f32), vmem((2, ZL, TILE, TILE), f32),
            vmem((8, TILE), f32), vmem((ZR, 8, TILE), f32), vmem((ZL, 8, TILE), f32),
            vmem((4, 8, TILE), f32), vmem((8, TILE), f32), vmem((8, TILE), f32),
            vmem((4, 8, TILE), f32), vmem((TILE, TILE), f32),
            vmem((16, COLS), f32), vmem((2, 2, TILE, TILE), f32),
            vmem((8, 16, COLS), f32), vmem((8, 16, COLS), f32),
            dma, dma, dma, dma, dma, dma, dma((3,)), dma((3,)),
            dma((3,)), dma((3,)), dma((3,)), dma((3,)),
            dma((ZR,)), dma((ZR,)), dma((ZL,)), dma((ZL,)),
            dma((2, ZR)), dma((2, ZR)), dma((2, ZL)), dma((2, ZL)),
            dma((ZR,)), dma((ZR,)), dma((ZL,)), dma((ZL,)),
            dma((3,)), dma((3,)), dma, dma, dma((3,)), dma((3,)),
            dma((33,)), dma((2,)),
        ],
        compiler_params=pltpu.CompilerParams(
            collective_id=0, has_side_effects=True, vmem_limit_bytes=48 << 20
        ),
        cost_estimate=pl.CostEstimate(flops=3_600_000_000, bytes_accessed=1_700_000, transcendentals=0),
        name="gram",
    )(snapshots)
    return strip.T


def solution(mesh):
    return jax.shard_map(
        per_device, mesh=mesh, in_specs=(P("rows", "snap"),), out_specs=P("snap", "rows"), check_vma=False
    )
```

time: 834 us -> 96.4 us (0.12)
  the two profiles are of different devices: /device:TPU:8 before, /device:TPU:9 now
where the time goes in v1:
time: 96.4 us; the launch traced here: 96.2 us
  Pallas kernels  94.2 us (98%)
  local copies, waits for them, and re-layouts  2.02 us (2%)
    pallas_call x1, Pallas kernels, per_device(): pl.pallas_call(kernel, out_shape=jax.ShapeDtypeStruct((16, COLS), f32), i...  94.2 us
    unnamed x3, local copies, waits for them, and re-layouts  2.02 us

profile of v1, /device:TPU:9, one launch (start us, length us, event | category | flops | bytes accessed | tf_op | source)
XLA Modules:
  0.0 96.2 jit_solution(14721385529584309743)
XLA Ops:
  0.0 0.0 copy-start
  0.0 1.4 %copy-done = f32[768,512]{1,0:T(8,128)S(1)} copy-done((f32[768,512]{1,0:T(8,128)S(1)}, f32[768,512]{1,0:T(8,128)}, u32[]{:S(2)}) %copy-start) | copy-done | bytes 1572888
  1.4 94.2 %gram.1 = f32[16,512]{1,0:T(8,128)S(1)} custom-call(f32[768,512]{1,0:T(8,128)S(1)} %copy-done), custom_call_target="tpu_custom_call" | custom-call | flops 3600000000 | bytes 1700000 | tf_op jit(solution)/shard_map/gram/pallas_call | solution.py:339
  95.6 0.6 copy.3
Async XLA Ops:
  0.0 1.4 %copy-start = (f32[768,512]{1,0:T(8,128)S(1)}, f32[768,512]{1,0:T(8,128)}, u32[]{:S(2)}) copy-start(f32[768,512]{1,0:T(8,128)} %x_ref.1) | copy-start | bytes 4718596

commit v2 on v1

--- a/solution.py
+++ b/solution.py
@@ -75,7 +75,11 @@
         send(sums.at[s], sums.at[s], sum_ss.at[i], sum_rs.at[i], target)
     send(x_ref, other, core_ss, core_rs, twin)
     give = pl.multiple_of((1 - low) * HALF, HALF)
-    send(x_ref.at[pl.ds(give, HALF)], cross.at[0], y_ss, y_rs, pair)
+    for e in range(2):
+        for q in range(HALF // TILE):
+            lanes = pl.ds(e * 256, 256)
+            send(x_ref.at[pl.ds(give + q * TILE, TILE), lanes], cross.at[0, pl.ds(q * TILE, TILE), lanes],
+                 y_ss.at[e, q], y_rs.at[e, q], pair)
 
     for i, d in enumerate((s ^ 1, s ^ 2, s ^ 3)):
         arrived(sums.at[d], sum_rs.at[i])
@@ -131,50 +135,36 @@
             got = product(t_hi[side, at, :], t_lo[side, at, :], hi[...], lo[...])
             aa[owner * 2 + half] = got.reshape(NZ, 16, COLS)
 
-    own_chip(0, core)
-    arrived(other, core_rs)
-    for q in range(ROWS // TILE):
+    keep = pl.multiple_of(low * HALF, HALF)
+
+    def relay(e, q):
+        piece = (pl.ds(q * TILE, TILE), pl.ds(e * 256, 256))
+        arrived(cross.at[(0,) + piece], y_rs.at[e, q])
+        send(cross.at[(0,) + piece], cross.at[(1,) + piece], relay_ss.at[e, q], relay_rs.at[e, q], twin)
+
+    def turn_cross(side, e, q):
         rows = slice(q * TILE, (q + 1) * TILE)
-        for j in range(4):
-            turn(other[rows, j * TILE:(j + 1) * TILE] - mean[rows, :], q, t_hi.at[1], t_lo.at[1], j)
-    own_chip(1, 1 - core)
-
-    a_half, b_half = pl.ds(0, ZR), pl.ds(ZR, ZR)
-    far, right, left = (x + 2) % NX, (x + 1) % NX, (x + NX - 1) % NX
-    send(aa.at[far, a_half], from_left.at[0], xr_ss.at[0], xr_rs.at[0], xr)
-    send(aa.at[far, b_half], from_right.at[0], xl_ss.at[0], xl_rs.at[0], xl)
-    send(aa.at[right, b_half], from_left.at[1], xr_ss.at[1], xr_rs.at[1], xr)
-    send(aa.at[left, a_half], from_right.at[1], xl_ss.at[1], xl_rs.at[1], xl)
-    for t in range(1, 4):
-        e_step(t)
-    arrived(from_left.at[0], xr_rs.at[0])
-    from_left[0] = from_left[0] + aa[right, a_half]
-    send(from_left.at[0], from_left.at[2], xr_ss.at[2], xr_rs.at[2], xr)
-    arrived(from_right.at[0], xl_rs.at[0])
-    from_right[0] = from_right[0] + aa[left, b_half]
-    send(from_right.at[0], from_right.at[2], xl_ss.at[2], xl_rs.at[2], xl)
-    for t in range(4, ZR + 1):
-        e_step(t)
-    e_x[3] = e_own[...] + jnp.sum(e_r[...], axis=0) + jnp.sum(e_l[...], axis=0)
-    for i, target in enumerate((xr, xl, xx)):
-        send(e_x.at[3], e_x.at[i], ex_ss.at[i], ex_rs.at[i], target)
-
-    keep = pl.multiple_of(low * HALF, HALF)
-
-    def cross_chip(side):
+        level = mean[pl.ds(keep + q * TILE, TILE), :]
+        for j in (2 * e, 2 * e + 1):
+            turn(cross[side, rows, j * TILE:(j + 1) * TILE] - level, q, c_hi.at[side], c_lo.at[side], j)
+
+    def place(side, g, lane):
+        index = side * 2 + lane // 2
+        return 8 * g + (index + 2 if lane % 2 == g else (index + 6) % 8)
+
+    def cross_chip(e):
         for q in range(HALF // TILE):
-            rows = slice(q * TILE, (q + 1) * TILE)
-            level = mean[pl.ds(keep + q * TILE, TILE), :]
-            for j in range(4):
-                turn(cross[side, rows, j * TILE:(j + 1) * TILE] - level, q, c_hi.at[side], c_lo.at[side], j)
-
-        @pl.loop(0, 4)
-        def _(tile):
-            at = pl.ds(pl.multiple_of(tile * TILE, TILE), TILE)
-            got = product(c_hi[side, at, :], c_lo[side, at, :],
-                          hi[pl.ds(keep, HALF), :], lo[pl.ds(keep, HALF), :])
-            for j in range(4):
-                ab[side, tile * 4 + j] = got[:, j * TILE:(j + 1) * TILE]
+            turn_cross(0, e, q)
+        for q in range(HALF // TILE):
+            arrived(cross.at[1, pl.ds(q * TILE, TILE), pl.ds(e * 256, 256)], relay_rs.at[e, q])
+            turn_cross(1, e, q)
+        for side in range(2):
+            for g in range(2):
+                at = slice((2 * e + g) * TILE, (2 * e + g + 1) * TILE)
+                got = product(c_hi[side, at, :], c_lo[side, at, :],
+                              hi[pl.ds(keep, HALF), :], lo[pl.ds(keep, HALF), :])
+                for j in range(4):
+                    ab[e, place(side, g, j)] = got[:, j * TILE:(j + 1) * TILE]
 
     def z_step(t, part, slots_r, slots_l, ssr, rsr, ssl, rsl):
         to_r, to_l = (z + ZR - t + NZ) % NZ, (z + NZ - ZL + t) % NZ
@@ -199,45 +189,153 @@
     def unit_step(t):
         z_step(t, unit, unit_r, unit_l, ur_ss, ur_rs, ul_ss, ul_rs)
 
-    def cross_step(t, side):
-        z_step(t, ab.at[side], ab_r.at[side], ab_l.at[side],
-               abr_ss.at[side], abr_rs.at[side], abl_ss.at[side], abl_rs.at[side])
-
-    arrived(cross.at[0], y_rs)
-    send(cross.at[0], cross.at[1], relay_ss, relay_rs, twin)
+    def cross_step(e, t):
+        z_step(t, ab.at[e], ab_r.at[e], ab_l.at[e], abr_ss.at[e], abr_rs.at[e], abl_ss.at[e], abl_rs.at[e])
+
+    a_half, b_half = pl.ds(0, ZR), pl.ds(ZR, ZR)
+    far, right, left = (x + 2) % NX, (x + 1) % NX, (x + NX - 1) % NX
+
+    def x_first():
+        send(aa.at[far, a_half], from_left.at[0], xr_ss.at[0], xr_rs.at[0], xr)
+        send(aa.at[far, b_half], from_right.at[0], xl_ss.at[0], xl_rs.at[0], xl)
+        send(aa.at[right, b_half], from_left.at[1], xr_ss.at[1], xr_rs.at[1], xr)
+        send(aa.at[left, a_half], from_right.at[1], xl_ss.at[1], xl_rs.at[1], xl)
+
+    def x_second():
+        arrived(from_left.at[0], xr_rs.at[0])
+        from_left[0] = from_left[0] + aa[right, a_half]
+        send(from_left.at[0], from_left.at[2], xr_ss.at[2], xr_rs.at[2], xr)
+        arrived(from_right.at[0], xl_rs.at[0])
+        from_right[0] = from_right[0] + aa[left, b_half]
+        send(from_right.at[0], from_right.at[2], xl_ss.at[2], xl_rs.at[2], xl)
+
+    def x_last():
+        for i in (1, 2):
+            arrived(from_left.at[i], xr_rs.at[i])
+            arrived(from_right.at[i], xl_rs.at[i])
+        unit[a_half] = aa[x, a_half] + from_left[2] + from_right[1]
+        unit[b_half] = aa[x, b_half] + from_left[1] + from_right[2]
+
+    def e_over_x():
+        e_x[3] = e_own[...] + jnp.sum(e_r[...], axis=0) + jnp.sum(e_l[...], axis=0)
+        for i, target in enumerate((xr, xl, xx)):
+            send(e_x.at[3], e_x.at[i], ex_ss.at[i], ex_rs.at[i], target)
+
+    def e_over_h():
+        for i in range(3):
+            arrived(e_x.at[i], ex_rs.at[i])
+        e_sum[...] = e_x[0] + e_x[1] + e_x[2] + e_x[3]
+        send(e_sum, e_h, eh_ss, eh_rs, hh)
+
+    def e_to_group():
+        arrived(e_h, eh_rs)
+        e_all[s] = e_sum[...] + e_h[...]
+        for i, target in enumerate(group):
+            send(e_all.at[s], e_all.at[s], eg_ss.at[i], eg_rs.at[i], target)
+
+    def e_done():
+        for i, d in enumerate((s ^ 1, s ^ 2, s ^ 3)):
+            arrived(e_all.at[d], eg_rs.at[i])
+
+    group8, spot = z // 8, z % 8
+    index = (spot + 2) % 4
+    middle = jnp.logical_and(spot >= 2, spot < 6)
+    lane_tile = (index % 2) * 2 + jnp.where(middle, group8, 1 - group8)
+    their = jnp.where(index // 2 == 0, core, 1 - core)
+    me = x * NH + h
+
+    def strip(e, k):
+        ox, oz = 2 * (1 - low) + their, group8 * 8 + k
+        own = jnp.logical_and(ox == x, jnp.logical_and(h == e, oz == z))
+        return own, device(ox, e, oz, low, core)
+
+    def cross_out(e):
+        block = z_last(ab.at[e], ab_r.at[e], ab_l.at[e], abr_rs.at[e], abl_rs.at[e])
+        flip[e, 0] = block
+        flip[e, 1] = block.T
+
+        @pl.loop(0, 8)
+        def _(k):
+            src = pl.ds(pl.multiple_of(k * 16, 16), 16)
+            lanes = pl.ds(pl.multiple_of(lane_tile * TILE, TILE), TILE)
+            own, owner = strip(e, k)
+
+            wide = pl.ds(pl.multiple_of((2 * e + group8) * TILE, TILE), TILE)
+            pltpu.make_async_remote_copy(
+                src_ref=flip.at[e, 1, src], dst_ref=turned.at[me, :, wide],
+                send_sem=fin_ss.at[9 + e * 16 + k], recv_sem=fin_rs.at[1],
+                device_id=device(2 * low + core, lane_tile // 2, (lane_tile % 2) * 8 + k, 1 - low, their),
+                device_id_type=MESH,
+            ).start()
+
+            @pl.when(own)
+            def _():
+                pltpu.make_async_copy(flip.at[e, 0, src], direct.at[me, :, lanes], fin_rs.at[0]).start()
+
+            @pl.when(jnp.logical_not(own))
+            def _():
+                pltpu.make_async_remote_copy(
+                    src_ref=flip.at[e, 0, src], dst_ref=direct.at[me, :, lanes],
+                    send_sem=fin_ss.at[1 + e * 16 + k], recv_sem=fin_rs.at[0],
+                    device_id=owner, device_id_type=MESH,
+                ).start()
+
+    own_chip(0, core)
+    relay(0, 0)
+    arrived(other, core_rs)
+    for q in range(ROWS // TILE):
+        rows = slice(q * TILE, (q + 1) * TILE)
+        for j in range(4):
+            turn(other[rows, j * TILE:(j + 1) * TILE] - mean[rows, :], q, t_hi.at[1], t_lo.at[1], j)
+    relay(0, 1)
+    own_chip(1, 1 - core)
+    x_first()
+    relay(0, 2)
+    e_step(1)
     cross_chip(0)
     cross_step(0, 0)
-
-    arrived(from_left.at[1], xr_rs.at[1])
-    arrived(from_right.at[1], xl_rs.at[1])
-    arrived(from_left.at[2], xr_rs.at[2])
-    arrived(from_right.at[2], xl_rs.at[2])
-    unit[a_half] = aa[x, a_half] + from_left[2] + from_right[1]
-    unit[b_half] = aa[x, b_half] + from_left[1] + from_right[2]
+    relay(1, 0)
+    e_step(2)
+    relay(1, 1)
+    e_step(3)
+    cross_step(0, 1)
+    e_step(4)
+    relay(1, 2)
+    x_second()
+    cross_step(0, 2)
+    e_step(5)
+    cross_chip(1)
+    cross_step(1, 0)
+    cross_step(0, 3)
+    e_step(6)
+    cross_step(1, 1)
+    cross_step(0, 4)
+    e_step(7)
+    cross_step(1, 2)
+    cross_step(0, 5)
+    e_step(8)
+    e_over_x()
+    x_last()
     unit_step(0)
-
-    arrived(cross.at[1], relay_rs)
-    cross_chip(1)
-    cross_step(0, 1)
-
-    for i in range(3):
-        arrived(e_x.at[i], ex_rs.at[i])
-    e_sum[...] = e_x[0] + e_x[1] + e_x[2] + e_x[3]
-    send(e_sum, e_h, eh_ss, eh_rs, hh)
-    for t in range(1, 3):
-        cross_step(t, 0)
-        unit_step(t)
-        cross_step(t, 1)
-    arrived(e_h, eh_rs)
-    e_all[s] = e_sum[...] + e_h[...]
-    for i, target in enumerate(group):
-        send(e_all.at[s], e_all.at[s], eg_ss.at[i], eg_rs.at[i], target)
-    for t in range(3, ZR):
-        cross_step(t, 0)
-        unit_step(t)
-        cross_step(t, 1)
-    for i, d in enumerate((s ^ 1, s ^ 2, s ^ 3)):
-        arrived(e_all.at[d], eg_rs.at[i])
+    cross_step(1, 3)
+    cross_step(0, 6)
+    unit_step(1)
+    e_over_h()
+    cross_step(1, 4)
+    cross_step(0, 7)
+    unit_step(2)
+    e_to_group()
+    cross_step(1, 5)
+    unit_step(3)
+    e_done()
+    cross_out(0)
+    cross_step(1, 6)
+    unit_step(4)
+    cross_step(1, 7)
+    unit_step(5)
+    cross_out(1)
+    unit_step(6)
+    unit_step(7)
 
     held[...] = z_last(unit, unit_r, unit_l, ur_rs, ul_rs)
     to_x, to_h = 2 * low + x // 2, x % 2
@@ -254,41 +352,6 @@
             device_id=device(to_x, to_h, z, low, core), device_id_type=MESH,
         ).start()
 
-    row_tile, lane_tile = z // 4, z % 4
-    me = x * NH + h
-    for side in range(2):
-        block = z_last(ab.at[side], ab_r.at[side], ab_l.at[side], abr_rs.at[side], abl_rs.at[side])
-        flip[side, 0] = block
-        flip[side, 1] = block.T
-        their = core if side == 0 else 1 - core
-
-        @pl.loop(0, 8)
-        def _(k):
-            src = pl.ds(pl.multiple_of(k * 16, 16), 16)
-            lanes = pl.ds(pl.multiple_of(lane_tile * TILE, TILE), TILE)
-            ox, oh, oz = 2 * (1 - low) + their, row_tile // 2, (row_tile % 2) * 8 + k
-            own = jnp.logical_and(ox == x, jnp.logical_and(oh == h, oz == z))
-
-            @pl.when(own)
-            def _():
-                pltpu.make_async_copy(flip.at[side, 0, src], direct.at[me, :, lanes], fin_rs.at[0]).start()
-
-            @pl.when(jnp.logical_not(own))
-            def _():
-                pltpu.make_async_remote_copy(
-                    src_ref=flip.at[side, 0, src], dst_ref=direct.at[me, :, lanes],
-                    send_sem=fin_ss.at[1 + side * 16 + k], recv_sem=fin_rs.at[0],
-                    device_id=device(ox, oh, oz, low, core), device_id_type=MESH,
-                ).start()
-
-            wide = pl.ds(pl.multiple_of(row_tile * TILE, TILE), TILE)
-            pltpu.make_async_remote_copy(
-                src_ref=flip.at[side, 1, src], dst_ref=turned.at[me, :, wide],
-                send_sem=fin_ss.at[9 + side * 16 + k], recv_sem=fin_rs.at[1],
-                device_id=device(2 * low + core, lane_tile // 2, (lane_tile % 2) * 8 + k, 1 - low, their),
-                device_id_type=MESH,
-            ).start()
-
     line = h * 2 + z // 8
     e_col[...] = jnp.broadcast_to(e_all[x, pl.ds(line, 1), :], (TILE, TILE)).T
     scale_j = lax.rsqrt(e_col[pl.ds(pl.multiple_of((z % 8) * 16, 16), 16), :] + eps)
@@ -317,20 +380,17 @@
     def _():
         arrived(held, fin_ss.at[0])
 
-    for side in range(2):
-        their = core if side == 0 else 1 - core
-
+    for e in range(2):
         @pl.loop(0, 8)
         def _(k):
-            src = flip.at[side, 0, pl.ds(0, 16)]
-            ox, oh, oz = 2 * (1 - low) + their, row_tile // 2, (row_tile % 2) * 8 + k
-            own = jnp.logical_and(ox == x, jnp.logical_and(oh == h, oz == z))
+            src = flip.at[e, 0, pl.ds(0, 16)]
+            own, _ = strip(e, k)
 
             @pl.when(jnp.logical_not(own))
             def _():
-                arrived(src, fin_ss.at[1 + side * 16 + k])
-
-            arrived(src, fin_ss.at[9 + side * 16 + k])
+                arrived(src, fin_ss.at[1 + e * 16 + k])
+
+            arrived(src, fin_ss.at[9 + e * 16 + k])
 
 
 def per_device(snapshots):
@@ -360,7 +420,7 @@
             vmem((4, 8, TILE), f32), vmem((TILE, TILE), f32),
             vmem((16, COLS), f32), vmem((2, 2, TILE, TILE), f32),
             vmem((8, 16, COLS), f32), vmem((8, 16, COLS), f32),
-            dma, dma, dma, dma, dma, dma, dma((3,)), dma((3,)),
+            dma, dma, dma((2, 3)), dma((2, 3)), dma((2, 3)), dma((2, 3)), dma((3,)), dma((3,)),
             dma((3,)), dma((3,)), dma((3,)), dma((3,)),
             dma((ZR,)), dma((ZR,)), dma((ZL,)), dma((ZL,)),
             dma((2, ZR)), dma((2, ZR)), dma((2, ZL)), dma((2, ZL)),

time: 96.4 us -> 86.2 us (0.89)
  the two profiles are of different devices: /device:TPU:9 before, /device:TPU:2 now
where the time goes in v2:
time: 86.2 us; the launch traced here: 86.1 us
  Pallas kernels  84.1 us (98%)
  local copies, waits for them, and re-layouts  2.02 us (2%)
    pallas_call x1, Pallas kernels, per_device(): pl.pallas_call(kernel, out_shape=jax.ShapeDtypeStruct((16, COLS), f32), i...  84.1 us
    unnamed x3, local copies, waits for them, and re-layouts  2.02 us

profile of v2, /device:TPU:2, one launch (start us, length us, event | category | flops | bytes accessed | tf_op | source)
XLA Modules:
  0.0 86.1 jit_solution(7114811829226194483)
XLA Ops:
  0.0 0.0 copy-start
  0.0 1.4 %copy-done = f32[768,512]{1,0:T(8,128)S(1)} copy-done((f32[768,512]{1,0:T(8,128)S(1)}, f32[768,512]{1,0:T(8,128)}, u32[]{:S(2)}) %copy-start) | copy-done | bytes 1572888
  1.4 84.1 %gram.1 = f32[16,512]{1,0:T(8,128)S(1)} custom-call(f32[768,512]{1,0:T(8,128)S(1)} %copy-done), custom_call_target="tpu_custom_call" | custom-call | flops 3600000000 | bytes 1700000 | tf_op jit(solution)/shard_map/gram/pallas_call | solution.py:399
  85.5 0.6 copy.3
Async XLA Ops:
  0.0 1.4 %copy-start = (f32[768,512]{1,0:T(8,128)S(1)}, f32[768,512]{1,0:T(8,128)}, u32[]{:S(2)}) copy-start(f32[768,512]{1,0:T(8,128)} %x_ref.1) | copy-start | bytes 4718596

commit v3 on v2

v3 whole, which is shorter than its diff:
```python
import jax
import jax.numpy as jnp
from jax import lax
from jax.experimental import pallas as pl
from jax.experimental.pallas import tpu as pltpu
from jax.sharding import PartitionSpec as P

eps = 1e-06
MESH = pl.DeviceIdType.MESH
f32, bf16 = jnp.float32, jnp.bfloat16

NX, NH, NZ = 4, 2, 16
ROWS, COLS = 768, 512
HALF = ROWS // 2
TILE = 128
SNAPS = 2048
SUB = 2
WIDE = 4 // SUB
ZR, ZL = NZ // 2, NZ // 2 - 1


def device(x, h, z, low, core):
    return ((x * NH + h) * NZ + z, low * 2 + core)


def kernel(
    x_hbm, out_ref,
    x_ref, other, cross, sums, mean, hi, lo, t_hi, t_lo, c_hi, c_lo,
    aa, ab, unit, from_left, from_right,
    unit_re, unit_ro, unit_lo, unit_le, aa_r, aa_l,
    e_own, e_x, e_z, e_g, e_all, e_col,
    held, flip, direct, turned,
    in_sem, core_ss, core_rs, y_ss, y_rs, relay_ss, relay_rs, sum_ss, sum_rs,
    xr_ss, xr_rs, xl_ss, xl_rs,
    ure_ss, ure_rs, uro_ss, uro_rs, ulo_ss, ulo_rs, ule_ss, ule_rs, aar_ss, aar_rs, aal_ss, aal_rs,
    ex_ss, ex_rs, ez_ss, ez_rs, eg_ss, eg_rs,
    own_ss, fin_ss, fin_rs,
):
    r, s = lax.axis_index("rows"), lax.axis_index("snap")
    x, h, z = r // (NH * NZ), (r // NZ) % NH, r % NZ
    low, core = s // 2, s % 2
    zr, zl = device(x, h, (z + 1) % NZ, low, core), device(x, h, (z + NZ - 1) % NZ, low, core)
    zr2, zl2 = device(x, h, (z + 2) % NZ, low, core), device(x, h, (z + NZ - 2) % NZ, low, core)
    xr, xl = device((x + 1) % NX, h, z, low, core), device((x + NX - 1) % NX, h, z, low, core)
    xx = device((x + 2) % NX, h, z, low, core)
    hh = device(x, 1 - h, z, low, core)
    twin = device(x, h, z, low, 1 - core)
    pair = device(x, h, z, 1 - low, core)
    diagonal = device(x, h, z, 1 - low, 1 - core)
    group = (twin, pair, diagonal)
    pending = []

    def send(src, dst, send_sem, recv_sem, target):
        copy = pltpu.make_async_remote_copy(
            src_ref=src, dst_ref=dst, send_sem=send_sem, recv_sem=recv_sem,
            device_id=target, device_id_type=MESH,
        )
        copy.start()
        pending.append((src, send_sem))
        return copy

    def arrived(dst, sem):
        pltpu.make_async_copy(dst, dst, sem).wait()

    def load(q):
        rows = pl.ds(q * TILE, TILE)
        return pltpu.make_async_copy(x_hbm.at[rows], x_ref.at[rows], in_sem.at[q])

    for q in range(ROWS // TILE):
        load(q).start()
    barrier = pltpu.get_barrier_semaphore()
    near = (twin, pair, diagonal, zr, zl, zr2, zl2, xr, xl, xx, hh)
    for target in near:
        pl.semaphore_signal(barrier, inc=1, device_id=target, device_id_type=MESH)

    def row_sums(q):
        load(q).wait()
        block = x_ref[q * TILE:(q + 1) * TILE, :]
        part = block[:, 0:128] + block[:, 128:256] + block[:, 256:384] + block[:, 384:512]
        sums[s, q:q + 1, :] = jnp.sum(part.T, axis=0, keepdims=True)

    for q in range(ROWS // TILE):
        row_sums(q)
    sums[s, 6:8, :] = jnp.zeros((2, TILE), f32)
    pl.semaphore_wait(barrier, len(near))

    for i, target in enumerate(group):
        send(sums.at[s], sums.at[s], sum_ss.at[i], sum_rs.at[i], target)
    give = pl.multiple_of((1 - low) * HALF, HALF)
    for e in range(2):
        for q in range(HALF // TILE):
            lanes = pl.ds(e * 256, 256)
            send(x_ref.at[pl.ds(give + q * TILE, TILE), lanes], cross.at[0, pl.ds(q * TILE, TILE), lanes],
                 y_ss.at[e, q], y_rs.at[e, q], pair)
        if e == 0:
            send(x_ref, other, core_ss, core_rs, twin)

    for i, d in enumerate((s ^ 1, s ^ 2, s ^ 3)):
        arrived(sums.at[d], sum_rs.at[i])
    mean_rows = (sums[0] + sums[1] + sums[2] + sums[3]) / SNAPS
    for q in range(ROWS // TILE):
        wide = jnp.broadcast_to(mean_rows[q:q + 1, :], (TILE, TILE))
        mean[q * TILE:(q + 1) * TILE, :] = wide.T

    def split(value):
        high = value.astype(bf16)
        return high, (value - high.astype(f32)).astype(bf16)

    def turn(block, q, to_hi, to_lo, j):
        high, rest = split(block.T)
        to_hi[j * TILE:(j + 1) * TILE, q * TILE:(q + 1) * TILE] = high
        to_lo[j * TILE:(j + 1) * TILE, q * TILE:(q + 1) * TILE] = rest

    energy = [jnp.zeros((8, TILE), f32) for _ in range(4)]
    for q in range(ROWS // TILE):
        rows = slice(q * TILE, (q + 1) * TILE)
        for j in range(4):
            block = x_ref[rows, j * TILE:(j + 1) * TILE] - mean[rows, :]
            energy[j] += jnp.sum((block * block).reshape(TILE // 8, 8, TILE), axis=0)
            high, rest = split(block)
            hi[rows, j * TILE:(j + 1) * TILE] = high
            lo[rows, j * TILE:(j + 1) * TILE] = rest
            turn(block, q, t_hi.at[0], t_lo.at[0], j)
    for j in range(4):
        e_own[j:j + 1, :] = jnp.sum(energy[j], axis=0, keepdims=True)
    e_own[4:8, :] = jnp.zeros((4, TILE), f32)

    z1 = device(x, h, z + 1 - 2 * (z % 2), low, core)
    z2 = device(x, h, z + 2 - 4 * ((z // 2) % 2), low, core)
    z4r, z4l = device(x, h, (z + 4) % NZ, low, core), device(x, h, (z + NZ - 4) % NZ, low, core)

    def e_step(t):
        if t == 0:
            for i, target in enumerate((xr, xl, xx)):
                send(e_own, e_x.at[i], ex_ss.at[i], ex_rs.at[i], target)
        elif t == 1:
            for i in range(3):
                arrived(e_x.at[i], ex_rs.at[i])
            e_z[0] = e_own[...] + e_x[0] + e_x[1] + e_x[2]
            send(e_z.at[0], e_g.at[0], ez_ss.at[0], ez_rs.at[0], hh)
        elif t in (2, 3, 4):
            arrived(e_g.at[t - 2], ez_rs.at[t - 2])
            e_z[t - 1] = e_z[t - 2] + e_g[t - 2]
            if t < 4:
                send(e_z.at[t - 1], e_g.at[t - 1], ez_ss.at[t - 1], ez_rs.at[t - 1], z1 if t == 2 else z2)
            else:
                send(e_z.at[3], e_g.at[3], ez_ss.at[3], ez_rs.at[3], z4r)
                send(e_z.at[3], e_g.at[4], ez_ss.at[4], ez_rs.at[4], z4l)
        elif t == 5:
            arrived(e_g.at[3], ez_rs.at[3])
            send(e_g.at[3], e_g.at[5], ez_ss.at[5], ez_rs.at[5], z4r)
            arrived(e_g.at[4], ez_rs.at[4])
        elif t == 6:
            arrived(e_g.at[5], ez_rs.at[5])
            e_all[s] = e_z[3] + e_g[3] + e_g[4] + e_g[5]
            for i, target in enumerate(group):
                send(e_all.at[s], e_all.at[s], eg_ss.at[i], eg_rs.at[i], target)
        else:
            for i, d in enumerate((s ^ 1, s ^ 2, s ^ 3)):
                arrived(e_all.at[d], eg_rs.at[i])

    e_step(0)

    def product(a_hi, a_lo, b_hi, b_lo):
        total = jnp.dot(a_hi, b_hi, preferred_element_type=f32)
        total += jnp.dot(a_hi, b_lo, preferred_element_type=f32)
        return total + jnp.dot(a_lo, b_hi, preferred_element_type=f32)

    def own_chip(side):
        got = product(t_hi[side], t_lo[side], hi[...], lo[...])
        for half in range(2):
            aa[:, side * 2 + half] = got[half * 256:(half + 1) * 256].reshape(NZ, 16, COLS)

    keep = pl.multiple_of(low * HALF, HALF)

    def relay(e, q):
        piece = (pl.ds(q * TILE, TILE), pl.ds(e * 256, 256))
        arrived(cross.at[(0,) + piece], y_rs.at[e, q])
        send(cross.at[(0,) + piece], cross.at[(1,) + piece], relay_ss.at[e, q], relay_rs.at[e, q], twin)

    def turn_cross(side, e, q):
        if side == 1:
            arrived(cross.at[1, pl.ds(q * TILE, TILE), pl.ds(e * 256, 256)], relay_rs.at[e, q])
        rows = slice(q * TILE, (q + 1) * TILE)
        level = mean[pl.ds(keep + q * TILE, TILE), :]
        for g in range(2):
            lanes = slice((2 * e + g) * TILE, (2 * e + g + 1) * TILE)
            turn(cross[side, rows, lanes] - level, q, c_hi.at[e], c_lo.at[e], side * 2 + g)

    def cross_chip(e):
        got = product(c_hi[e], c_lo[e], hi[pl.ds(keep, HALF), :], lo[pl.ds(keep, HALF), :])
        for side in range(2):
            for g in range(2):
                for j in range(4):
                    for k in range(4):
                        at = (side * 2 + g) * TILE + k * 32
                        ab[e, j, 8 * g + 2 * k + side] = got[at:at + 32, j * TILE:(j + 1) * TILE]

    def hop(t, part, slots, ss, rs, target):
        src = part if t == 0 else slots.at[t - 1]
        if t > 0:
            arrived(slots.at[t - 1], rs.at[t - 1])
            slots[t - 1] = slots[t - 1] + part[...]
        send(src, slots.at[t], ss.at[t], rs.at[t], target)

    def unit_step(e, t):
        def one(distance, slots, ss, rs, target):
            hop(t, unit.at[e, (z + distance) % NZ], slots.at[e], ss.at[e], rs.at[e], target)

        one(8 - 2 * t, unit_re, ure_ss, ure_rs, zr2)
        one(9 + 2 * t, unit_lo, ulo_ss, ulo_rs, zl2 if t < 3 else zl)
        one(7 - 2 * t, unit_ro, uro_ss, uro_rs, zr2 if t < 3 else zr)
        if t < 3:
            one(10 + 2 * t, unit_le, ule_ss, ule_rs, zl2)

    def unit_last(e):
        total = unit[e, z]
        for slots, rs, n in ((unit_le, ule_rs, 3), (unit_re, ure_rs, 4), (unit_ro, uro_rs, 4), (unit_lo, ulo_rs, 4)):
            arrived(slots.at[e, n - 1], rs.at[e, n - 1])
            total = total + slots[e, n - 1]
        return total

    def own_step(u, t):
        half = pl.ds(WIDE * u, WIDE)
        if t < ZR:
            hop(t, aa.at[(z + ZR - t) % NZ, half], aa_r.at[u], aar_ss.at[u], aar_rs.at[u], zr)
        if t < ZL:
            hop(t, aa.at[(z + NZ - ZL + t) % NZ, half], aa_l.at[u], aal_ss.at[u], aal_rs.at[u], zl)

    def own_owner(u):
        ox, oh = 2 * low + (core if u < 2 else 1 - core), u % 2
        return jnp.logical_and(ox == x, oh == h), device(ox, oh, z, low, core)

    def own_out():
        for u in range(SUB):
            arrived(aa_r.at[u, ZR - 1], aar_rs.at[u, ZR - 1])
            arrived(aa_l.at[u, ZL - 1], aal_rs.at[u, ZL - 1])
            half = pl.ds(WIDE * u, WIDE)
            held[half] = aa[z, half] + aa_r[u, ZR - 1] + aa_l[u, ZL - 1]
        for u in range(4):
            mine, owner = own_owner(u)

            @pl.when(mine)
            def _():
                pltpu.make_async_copy(held.at[u], direct.at[me], fin_rs.at[0]).start()

            @pl.when(jnp.logical_not(mine))
            def _():
                pltpu.make_async_remote_copy(
                    src_ref=held.at[u], dst_ref=direct.at[me], send_sem=own_ss.at[u], recv_sem=fin_rs.at[0],
                    device_id=owner, device_id_type=MESH,
                ).start()

    a_half, b_half = pl.ds(0, ZR), pl.ds(ZR, ZR)
    far, right, left = (x + 2) % NX, (x + 1) % NX, (x + NX - 1) % NX

    def x_first(e):
        part, by_l, by_r = ab.at[e], from_left.at[e], from_right.at[e]
        send(part.at[far, a_half], by_l.at[0], xr_ss.at[e, 0], xr_rs.at[e, 0], xr)
        send(part.at[far, b_half], by_r.at[0], xl_ss.at[e, 0], xl_rs.at[e, 0], xl)
        send(part.at[right, b_half], by_l.at[1], xr_ss.at[e, 1], xr_rs.at[e, 1], xr)
        send(part.at[left, a_half], by_r.at[1], xl_ss.at[e, 1], xl_rs.at[e, 1], xl)

    def x_second(e):
        part, by_l, by_r = ab.at[e], from_left.at[e], from_right.at[e]
        arrived(by_l.at[0], xr_rs.at[e, 0])
        by_l[0] = by_l[0] + part[right, a_half]
        send(by_l.at[0], by_l.at[2], xr_ss.at[e, 2], xr_rs.at[e, 2], xr)
        arrived(by_r.at[0], xl_rs.at[e, 0])
        by_r[0] = by_r[0] + part[left, b_half]
        send(by_r.at[0], by_r.at[2], xl_ss.at[e, 2], xl_rs.at[e, 2], xl)

    def x_last(e):
        for i in (1, 2):
            arrived(from_left.at[e, i], xr_rs.at[e, i])
            arrived(from_right.at[e, i], xl_rs.at[e, i])
        unit[e, a_half] = ab[e, x, a_half] + from_left[e, 2] + from_right[e, 1]
        unit[e, b_half] = ab[e, x, b_half] + from_left[e, 1] + from_right[e, 2]

    group8, quarter = z // 8, (z % 8) // 2
    their = jnp.where(z % 2 == 0, core, 1 - core)
    me = x * NH + h

    def strip(e, k):
        ox, oz = 2 * (1 - low) + their, group8 * 8 + quarter * 2 + k
        own = jnp.logical_and(ox == x, jnp.logical_and(h == e, oz == z))
        return own, device(ox, e, oz, low, core)

    def cross_out(e):
        block = unit_last(e)
        flip[e, 0, 0:32, :] = block
        column = lax.broadcasted_iota(jnp.int32, (TILE, TILE), 1)
        tall = jnp.concatenate([block] * 4, axis=0).T
        flip[e, 1] = jnp.where(column // 32 == quarter, tall, 0.0)
        wide = pl.ds(pl.multiple_of((2 * e + group8) * TILE, TILE), TILE)
        lanes = pl.ds(pl.multiple_of(x * TILE, TILE), TILE)

        @pl.loop(0, 8)
        def _(k):
            src = pl.ds(pl.multiple_of(k * 16, 16), 16)
            pltpu.make_async_remote_copy(
                src_ref=flip.at[e, 1, src], dst_ref=turned.at[quarter * 2 + h, :, wide],
                send_sem=fin_ss.at[e, 2 + k], recv_sem=fin_rs.at[1],
                device_id=device(2 * low + core, x // 2, (x % 2) * 8 + k, 1 - low, their),
                device_id_type=MESH,
            ).start()

        for k in range(2):
            src = pl.ds(k * 16, 16)
            own, owner = strip(e, k)

            @pl.when(own)
            def _():
                pltpu.make_async_copy(flip.at[e, 0, src], direct.at[h, :, lanes], fin_rs.at[0]).start()

            @pl.when(jnp.logical_not(own))
            def _():
                pltpu.make_async_remote_copy(
                    src_ref=flip.at[e, 0, src], dst_ref=direct.at[h, :, lanes],
                    send_sem=fin_ss.at[e, k], recv_sem=fin_rs.at[0],
                    device_id=owner, device_id_type=MESH,
                ).start()

    def other_chip():
        arrived(other, core_rs)
        for q in range(ROWS // TILE):
            rows = slice(q * TILE, (q + 1) * TILE)
            for j in range(4):
                turn(other[rows, j * TILE:(j + 1) * TILE] - mean[rows, :], q, t_hi.at[1], t_lo.at[1], j)

    own_chip(0)
    relay(0, 0)
    other_chip()
    relay(0, 1)
    own_chip(1)
    for u in range(SUB): own_step(u, 0)
    relay(0, 2)
    turn_cross(0, 0, 0)
    turn_cross(0, 0, 1)
    turn_cross(0, 0, 2)
    turn_cross(1, 0, 0)
    turn_cross(1, 0, 1)
    turn_cross(1, 0, 2)
    e_step(1)
    cross_chip(0)
    x_first(0)
    for u in range(SUB): own_step(u, 1)
    relay(1, 0)
    turn_cross(0, 1, 0)
    e_step(2)
    relay(1, 1)
    turn_cross(0, 1, 1)
    turn_cross(1, 1, 0)
    turn_cross(1, 1, 1)
    for u in range(SUB): own_step(u, 2)
    x_second(0)
    relay(1, 2)
    turn_cross(0, 1, 2)
    turn_cross(1, 1, 2)
    e_step(3)
    cross_chip(1)
    x_first(1)
    for u in range(SUB): own_step(u, 3)
    x_last(0)
    unit_step(0, 0)
    x_second(1)
    for u in range(SUB): own_step(u, 4)
    unit_step(0, 1)
    e_step(4)
    for u in range(SUB): own_step(u, 5)
    unit_step(0, 2)
    x_last(1)
    unit_step(1, 0)
    e_step(5)
    for u in range(SUB): own_step(u, 6)
    unit_step(0, 3)
    unit_step(1, 1)
    e_step(6)
    for u in range(SUB): own_step(u, 7)
    e_step(7)
    cross_out(0)
    unit_step(1, 2)
    own_out()
    unit_step(1, 3)
    cross_out(1)

    line = h * 2 + z // 8
    e_col[...] = jnp.broadcast_to(e_all[x, pl.ds(line, 1), :], (TILE, TILE)).T
    scale_j = lax.rsqrt(e_col[pl.ds(pl.multiple_of((z % 8) * 16, 16), 16), :] + eps)
    scale_i = lax.rsqrt(e_all[s] + eps)

    def finish(total):
        for j in range(4):
            lanes = slice(j * TILE, (j + 1) * TILE)
            out_ref[:, lanes] = total[:, lanes] * scale_i[j:j + 1, :] * scale_j

    for src, sem in pending:
        arrived(src, sem)

    @pl.when(x // 2 == low)
    def _():
        arrived(direct, fin_rs.at[0])
        finish(jnp.sum(direct[...], axis=0))

    @pl.when(x // 2 != low)
    def _():
        arrived(direct.at[pl.ds(0, 2)], fin_rs.at[0])
        arrived(turned, fin_rs.at[1])
        finish(direct[0] + direct[1] + jnp.sum(turned[...], axis=0))

    for u in range(4):
        mine, _ = own_owner(u)

        @pl.when(jnp.logical_not(mine))
        def _():
            arrived(held.at[u], own_ss.at[u])

    for e in range(2):
        src = flip.at[e, 0, pl.ds(0, 16)]
        for k in range(2):
            own, _ = strip(e, k)

            @pl.when(jnp.logical_not(own))
            def _():
                arrived(src, fin_ss.at[e, k])

        @pl.loop(0, 8)
        def _(k):
            arrived(src, fin_ss.at[e, 2 + k])


def per_device(snapshots):
    dma = pltpu.SemaphoreType.DMA
    vmem = pltpu.VMEM
    strip = pl.pallas_call(
        kernel,
        out_shape=jax.ShapeDtypeStruct((16, COLS), f32),
        in_specs=[pl.BlockSpec(memory_space=pl.ANY)],
        out_specs=pl.BlockSpec(memory_space=pltpu.VMEM),
        scratch_shapes=[
            vmem((ROWS, COLS), f32), vmem((ROWS, COLS), f32),
            vmem((2, HALF, COLS), f32),
            vmem((4, 8, TILE), f32),
            vmem((ROWS, TILE), f32),
            vmem((ROWS, COLS), bf16), vmem((ROWS, COLS), bf16),
            vmem((2, COLS, ROWS), bf16), vmem((2, COLS, ROWS), bf16),
            vmem((2, COLS, HALF), bf16), vmem((2, COLS, HALF), bf16),
            vmem((NZ, 4, 16, COLS), f32),
            vmem((2, NX, NZ, 32, TILE), f32),
            vmem((2, NZ, 32, TILE), f32),
            vmem((2, 3, ZR, 32, TILE), f32), vmem((2, 3, ZR, 32, TILE), f32),
            vmem((2, 4, 32, TILE), f32), vmem((2, 4, 32, TILE), f32),
            vmem((2, 4, 32, TILE), f32), vmem((2, 3, 32, TILE), f32),
            vmem((SUB, ZR, WIDE, 16, COLS), f32), vmem((SUB, ZL, WIDE, 16, COLS), f32),
            vmem((8, TILE), f32), vmem((3, 8, TILE), f32),
            vmem((4, 8, TILE), f32), vmem((6, 8, TILE), f32),
            vmem((4, 8, TILE), f32), vmem((TILE, TILE), f32),
            vmem((4, 16, COLS), f32), vmem((2, 2, TILE, TILE), f32),
            vmem((8, 16, COLS), f32), vmem((8, 16, COLS), f32),
            dma((6,)), dma, dma, dma((2, 3)), dma((2, 3)), dma((2, 3)), dma((2, 3)), dma((3,)), dma((3,)),
            dma((2, 3)), dma((2, 3)), dma((2, 3)), dma((2, 3)),
            dma((2, 4)), dma((2, 4)), dma((2, 4)), dma((2, 4)), dma((2, 4)), dma((2, 4)), dma((2, 3)), dma((2, 3)),
            dma((SUB, ZR)), dma((SUB, ZR)), dma((SUB, ZL)), dma((SUB, ZL)),
            dma((3,)), dma((3,)), dma((6,)), dma((6,)), dma((3,)), dma((3,)),
            dma((4,)), dma((2, 10)), dma((2,)),
        ],
        compiler_params=pltpu.CompilerParams(
            collective_id=0, has_side_effects=True, vmem_limit_bytes=48 << 20
        ),
        cost_estimate=pl.CostEstimate(flops=3_600_000_000, bytes_accessed=1_700_000, transcendentals=0),
        name="gram",
    )(snapshots)
    return strip.T


def solution(mesh):
    return jax.shard_map(
        per_device, mesh=mesh, in_specs=(P("rows", "snap"),), out_specs=P("snap", "rows"), check_vma=False
    )
```

time: 86.2 us -> 84.2 us (0.977)
  the two profiles are of different devices: /device:TPU:2 before, /device:TPU:5 now
where the time goes in v3:
time: 84.2 us; the launch traced here: 84 us
  Pallas kernels  82 us (97%)
  local copies, waits for them, and re-layouts  2.02 us (2%)
    pallas_call x1, Pallas kernels, per_device(): pl.pallas_call(kernel, out_shape=jax.ShapeDtypeStruct((16, COLS), f32), i...  82 us
    unnamed x3, local copies, waits for them, and re-layouts  2.02 us

profile of v3, /device:TPU:5, one launch (start us, length us, event | category | flops | bytes accessed | tf_op | source)
XLA Modules:
  0.0 84.0 jit_solution(18418403682199768320)
XLA Ops:
  0.0 0.0 copy-start
  0.0 1.4 %copy-done = f32[768,512]{1,0:T(8,128)S(1)} copy-done((f32[768,512]{1,0:T(8,128)S(1)}, f32[768,512]{1,0:T(8,128)}, u32[]{:S(2)}) %copy-start) | copy-done | bytes 1572888
  1.4 82.0 %gram.1 = f32[16,512]{1,0:T(8,128)S(1)} custom-call(f32[768,512]{1,0:T(8,128)S(1)} %copy-done), custom_call_target="tpu_custom_call" | custom-call | flops 3600000000 | bytes 1700000 | tf_op jit(solution)/shard_map/gram/pallas_call | solution.py:435
  83.4 0.6 copy.3
Async XLA Ops:
  0.0 1.4 %copy-start = (f32[768,512]{1,0:T(8,128)S(1)}, f32[768,512]{1,0:T(8,128)}, u32[]{:S(2)}) copy-start(f32[768,512]{1,0:T(8,128)} %x_hbm.1) | copy-start | bytes 4718596

commit v4 on v3

--- a/solution.py
+++ b/solution.py
@@ -131,21 +131,26 @@
 
     def e_step(t):
         if t == 0:
+            send(e_own, e_g.at[0], ez_ss.at[0], ez_rs.at[0], z1)
+        elif t == 1:
+            arrived(e_g.at[0], ez_rs.at[0])
+            e_z[0] = e_own[...] + e_g[0]
+            send(e_z.at[0], e_g.at[1], ez_ss.at[1], ez_rs.at[1], z2)
+        elif t == 2:
+            arrived(e_g.at[1], ez_rs.at[1])
+            e_z[1] = e_z[0] + e_g[1]
             for i, target in enumerate((xr, xl, xx)):
-                send(e_own, e_x.at[i], ex_ss.at[i], ex_rs.at[i], target)
-        elif t == 1:
+                send(e_z.at[1], e_x.at[i], ex_ss.at[i], ex_rs.at[i], target)
+        elif t == 3:
             for i in range(3):
                 arrived(e_x.at[i], ex_rs.at[i])
-            e_z[0] = e_own[...] + e_x[0] + e_x[1] + e_x[2]
-            send(e_z.at[0], e_g.at[0], ez_ss.at[0], ez_rs.at[0], hh)
-        elif t in (2, 3, 4):
-            arrived(e_g.at[t - 2], ez_rs.at[t - 2])
-            e_z[t - 1] = e_z[t - 2] + e_g[t - 2]
-            if t < 4:
-                send(e_z.at[t - 1], e_g.at[t - 1], ez_ss.at[t - 1], ez_rs.at[t - 1], z1 if t == 2 else z2)
-            else:
-                send(e_z.at[3], e_g.at[3], ez_ss.at[3], ez_rs.at[3], z4r)
-                send(e_z.at[3], e_g.at[4], ez_ss.at[4], ez_rs.at[4], z4l)
+            e_z[2] = e_z[1] + e_x[0] + e_x[1] + e_x[2]
+            send(e_z.at[2], e_g.at[2], ez_ss.at[2], ez_rs.at[2], hh)
+        elif t == 4:
+            arrived(e_g.at[2], ez_rs.at[2])
+            e_z[3] = e_z[2] + e_g[2]
+            send(e_z.at[3], e_g.at[3], ez_ss.at[3], ez_rs.at[3], z4r)
+            send(e_z.at[3], e_g.at[4], ez_ss.at[4], ez_rs.at[4], z4l)
         elif t == 5:
             arrived(e_g.at[3], ez_rs.at[3])
             send(e_g.at[3], e_g.at[5], ez_ss.at[5], ez_rs.at[5], z4r)
@@ -329,60 +334,68 @@
                 turn(other[rows, j * TILE:(j + 1) * TILE] - mean[rows, :], q, t_hi.at[1], t_lo.at[1], j)
 
     own_chip(0)
+    own_step(0, 0)
     relay(0, 0)
     other_chip()
+    e_step(1)
     relay(0, 1)
+    own_step(0, 1)
     own_chip(1)
-    for u in range(SUB): own_step(u, 0)
+    own_step(1, 0)
+    e_step(2)
     relay(0, 2)
+    own_step(0, 2)
     turn_cross(0, 0, 0)
     turn_cross(0, 0, 1)
     turn_cross(0, 0, 2)
     turn_cross(1, 0, 0)
     turn_cross(1, 0, 1)
     turn_cross(1, 0, 2)
-    e_step(1)
     cross_chip(0)
     x_first(0)
-    for u in range(SUB): own_step(u, 1)
+    own_step(1, 1)
+    own_step(0, 3)
     relay(1, 0)
     turn_cross(0, 1, 0)
-    e_step(2)
     relay(1, 1)
+    e_step(3)
+    own_step(1, 2)
     turn_cross(0, 1, 1)
     turn_cross(1, 1, 0)
     turn_cross(1, 1, 1)
-    for u in range(SUB): own_step(u, 2)
+    own_step(0, 4)
     x_second(0)
     relay(1, 2)
     turn_cross(0, 1, 2)
     turn_cross(1, 1, 2)
-    e_step(3)
     cross_chip(1)
     x_first(1)
-    for u in range(SUB): own_step(u, 3)
+    own_step(1, 3)
+    own_step(0, 5)
     x_last(0)
     unit_step(0, 0)
+    own_step(1, 4)
     x_second(1)
-    for u in range(SUB): own_step(u, 4)
+    own_step(0, 6)
     unit_step(0, 1)
     e_step(4)
-    for u in range(SUB): own_step(u, 5)
+    own_step(1, 5)
+    own_step(0, 7)
     unit_step(0, 2)
     x_last(1)
     unit_step(1, 0)
+    own_step(1, 6)
+    unit_step(0, 3)
     e_step(5)
-    for u in range(SUB): own_step(u, 6)
-    unit_step(0, 3)
     unit_step(1, 1)
-    e_step(6)
-    for u in range(SUB): own_step(u, 7)
-    e_step(7)
+    own_step(1, 7)
     cross_out(0)
     unit_step(1, 2)
+    e_step(6)
     own_out()
     unit_step(1, 3)
     cross_out(1)
+    e_step(7)
 
     line = h * 2 + z // 8
     e_col[...] = jnp.broadcast_to(e_all[x, pl.ds(line, 1), :], (TILE, TILE)).T

time: 84.2 us -> 81.4 us (0.967)
  Pallas kernels: 82 us -> 79.2 us
    pallas_call x1, Pallas kernels: 82 us -> 79.2 us  [per_device(): pl.pallas_call(kernel, out_shape=jax.ShapeDtypeStruct((16, COLS), f32), i...]
where the time goes in v4:
time: 81.4 us; the launch traced here: 81.2 us
  Pallas kernels  79.2 us (97%)
  local copies, waits for them, and re-layouts  2.02 us (2%)
    pallas_call x1, Pallas kernels, per_device(): pl.pallas_call(kernel, out_shape=jax.ShapeDtypeStruct((16, COLS), f32), i...  79.2 us
    unnamed x3, local copies, waits for them, and re-layouts  2.02 us

profile of v4, /device:TPU:5, one launch (start us, length us, event | category | flops | bytes accessed | tf_op | source)
XLA Modules:
  0.0 81.2 jit_solution(11066999337790389727)
XLA Ops:
  0.0 0.0 copy-start
  0.0 1.4 %copy-done = f32[768,512]{1,0:T(8,128)S(1)} copy-done((f32[768,512]{1,0:T(8,128)S(1)}, f32[768,512]{1,0:T(8,128)}, u32[]{:S(2)}) %copy-start) | copy-done | bytes 1572888
  1.4 79.2 %gram.1 = f32[16,512]{1,0:T(8,128)S(1)} custom-call(f32[768,512]{1,0:T(8,128)S(1)} %copy-done), custom_call_target="tpu_custom_call" | custom-call | flops 3600000000 | bytes 1700000 | tf_op jit(solution)/shard_map/gram/pallas_call | solution.py:448
  80.6 0.6 copy.3
Async XLA Ops:
  0.0 1.4 %copy-start = (f32[768,512]{1,0:T(8,128)S(1)}, f32[768,512]{1,0:T(8,128)}, u32[]{:S(2)}) copy-start(f32[768,512]{1,0:T(8,128)} %x_hbm.1) | copy-start | bytes 4718596

commit v5 on v4

--- a/solution.py
+++ b/solution.py
@@ -300,9 +300,8 @@
         wide = pl.ds(pl.multiple_of((2 * e + group8) * TILE, TILE), TILE)
         lanes = pl.ds(pl.multiple_of(x * TILE, TILE), TILE)
 
-        @pl.loop(0, 8)
-        def _(k):
-            src = pl.ds(pl.multiple_of(k * 16, 16), 16)
+        for k in range(8):
+            src = pl.ds(k * 16, 16)
             pltpu.make_async_remote_copy(
                 src_ref=flip.at[e, 1, src], dst_ref=turned.at[quarter * 2 + h, :, wide],
                 send_sem=fin_ss.at[e, 2 + k], recv_sem=fin_rs.at[1],
@@ -437,8 +436,7 @@
             def _():
                 arrived(src, fin_ss.at[e, k])
 
-        @pl.loop(0, 8)
-        def _(k):
+        for k in range(8):
             arrived(src, fin_ss.at[e, 2 + k])
 
 

time: 81.4 us -> 81.2 us (level)
  no operation moved by 1% of the time
where the time goes in v5:
time: 81.2 us; the launch traced here: 81.1 us
  Pallas kernels  79.1 us (97%)
  local copies, waits for them, and re-layouts  2.02 us (2%)
    pallas_call x1, Pallas kernels, per_device(): pl.pallas_call(kernel, out_shape=jax.ShapeDtypeStruct((16, COLS), f32), i...  79.1 us
    unnamed x3, local copies, waits for them, and re-layouts  2.02 us

profile of v5, /device:TPU:5, one launch (start us, length us, event | category | flops | bytes accessed | tf_op | source)
XLA Modules:
  0.0 81.1 jit_solution(15824410391082666831)
XLA Ops:
  0.0 0.0 copy-start
  0.0 1.4 %copy-done = f32[768,512]{1,0:T(8,128)S(1)} copy-done((f32[768,512]{1,0:T(8,128)S(1)}, f32[768,512]{1,0:T(8,128)}, u32[]{:S(2)}) %copy-start) | copy-done | bytes 1572888
  1.4 79.1 %gram.1 = f32[16,512]{1,0:T(8,128)S(1)} custom-call(f32[768,512]{1,0:T(8,128)S(1)} %copy-done), custom_call_target="tpu_custom_call" | custom-call | flops 3600000000 | bytes 1700000 | tf_op jit(solution)/shard_map/gram/pallas_call | solution.py:446
  80.5 0.6 copy.3
Async XLA Ops:
  0.0 1.4 %copy-start = (f32[768,512]{1,0:T(8,128)S(1)}, f32[768,512]{1,0:T(8,128)}, u32[]{:S(2)}) copy-start(f32[768,512]{1,0:T(8,128)} %x_hbm.1) | copy-start | bytes 4718596
